TPU v7x, 32 devices: a whole 2x2x4 slice. The times are simulated.
32 devices in a mesh: expert: 4 (over z), dp: 2 (over y), tensor: 4 (over x, core).
Axes of the slice: x: 2, y: 2, z: 4, core: 2. Of those that a mesh axis runs over, the one named last changes fastest.
Arguments:
- tokens: bfloat16 [1024, 4096], P(('expert', 'dp')), may hold values from -6 to 6
- out_grad: bfloat16 [1024, 4096], P(('expert', 'dp')), may hold values from -1.1953125 to 1.1953125
- expert_index: int32 [1024, 2], P(('expert', 'dp')), may hold values from 0 to 3, as said below
- slot_index: int32 [1024, 2], P(('expert', 'dp')), may hold values from 0 to 95, as said below
- gate_probs: float32 [1024, 2], P(('expert', 'dp')), may hold values from 0.05 to 0.95
- gate_weight: bfloat16 [4, 4096, 2048], P('expert', None, 'tensor'), may hold values from -0.09375 to 0.09375
- up_weight: bfloat16 [4, 4096, 2048], P('expert', None, 'tensor'), may hold values from -0.09375 to 0.09375
- down_weight: bfloat16 [4, 2048, 4096], P('expert', 'tensor'), may hold values from -0.125 to 0.125
Outputs:
- token_grad: bfloat16 [1024, 4096], P(('expert', 'dp'), 'tensor')
- gate_grad: bfloat16 [4, 4096, 2048], P('expert', 'dp', 'tensor')
- up_grad: bfloat16 [4, 4096, 2048], P('expert', 'dp', 'tensor')
- down_grad: bfloat16 [4, 2048, 4096], P('expert', 'tensor', 'dp')
Inputs may be any that keep to these rules, and one draw needn't show every extreme that they name: `expert_index`: in each block of 128 rows (the rows of one device) the two experts of a row differ; in every block one expert is named by exactly 96 rows and no expert by more, and that expert is the same for all blocks of one group. `slot_index`: within one block, the choices that name one expert carry distinct slots that run from 0 to their number minus one; a choice whose slot is 48 or more is dropped.
All inputs are finite; a program needn't handle non-finite values.
Results may differ from a plain program's by a relative error of at most 0.014.
Values may be sent and summed in bfloat16 or wider, within the bound.
A program may use at most 64 MiB of HBM per device.

v0:
```python
import jax
import jax.numpy as jnp
from jax import lax
from jax.sharding import PartitionSpec as P


def on_device(
    tokens, out_grad, expert_index, slot_index, gate_probs, gate_weight, up_weight, down_weight
):
    local_rows, model_width = tokens.shape
    experts = lax.axis_size("expert")
    capacity = 3 * local_rows // (2 * experts)
    slot_count = experts * capacity
    kept_mask = slot_index < capacity
    target = jnp.where(kept_mask, expert_index * capacity + slot_index, slot_count)
    owners = jnp.repeat(jnp.arange(local_rows, dtype=jnp.int32), 2)
    source_row = (
        jnp.full((slot_count + 1,), local_rows, jnp.int32)
        .at[target.reshape(-1)]
        .set(owners)[:slot_count]
    )
    slot_prob = (
        jnp.zeros((slot_count + 1,), jnp.float32)
        .at[target.reshape(-1)]
        .set(gate_probs.reshape(-1))[:slot_count]
    )
    send_tokens = jnp.take(tokens, source_row, axis=0, mode="fill", fill_value=0)
    send_grads = (
        slot_prob[:, None] * jnp.take(out_grad, source_row, axis=0, mode="fill", fill_value=0)
    ).astype(jnp.bfloat16)
    tensor_part = model_width // lax.axis_size("tensor")
    offset = lax.axis_index("tensor") * tensor_part
    token_share = lax.dynamic_slice_in_dim(send_tokens, offset, tensor_part, 1)
    grad_share = lax.dynamic_slice_in_dim(send_grads, offset, tensor_part, 1)
    token_share, grad_share = (
        lax.all_to_all(token_share, "expert", split_axis=0, concat_axis=0, tiled=True),
        lax.all_to_all(grad_share, "expert", split_axis=0, concat_axis=0, tiled=True),
    )
    routed, scaled = (
        lax.all_gather(token_share, "tensor", axis=1, tiled=True),
        lax.all_gather(grad_share, "tensor", axis=1, tiled=True),
    )
    gate_matrix = gate_weight[0]
    up_matrix = up_weight[0]
    down_matrix = down_weight[0]
    contract_last = (((1,), (1,)), ((), ()))
    gate_value = jnp.dot(routed, gate_matrix, preferred_element_type=jnp.float32)
    up_value = jnp.dot(routed, up_matrix, preferred_element_type=jnp.float32)
    gate_sigmoid = jax.nn.sigmoid(gate_value)
    activated = gate_value * gate_sigmoid
    hidden = (activated * up_value).astype(jnp.bfloat16)
    back_grad = lax.dot_general(
        scaled, down_matrix, contract_last, preferred_element_type=jnp.float32
    )
    gate_delta = (
        back_grad * up_value * gate_sigmoid * (1.0 + gate_value * (1.0 - gate_sigmoid))
    ).astype(jnp.bfloat16)
    up_delta = (back_grad * activated).astype(jnp.bfloat16)
    gate_rows = gate_matrix
    up_rows = up_matrix
    gate_term = lax.dot_general(
        gate_rows, gate_delta, contract_last, preferred_element_type=jnp.float32
    )
    summed = lax.psum_scatter(
        gate_term
        + lax.dot_general(up_rows, up_delta, contract_last, preferred_element_type=jnp.float32),
        "tensor",
        scatter_dimension=0,
        tiled=True,
    )
    returned = lax.all_to_all(
        summed.reshape(tensor_part, experts, capacity),
        "expert",
        split_axis=1,
        concat_axis=1,
        tiled=True,
    )
    slot_rows = jnp.transpose(returned.reshape(tensor_part, slot_count))
    safe_target = jnp.minimum(target, slot_count - 1)
    chosen = jnp.take(slot_rows, safe_target.reshape(-1), axis=0).reshape(
        local_rows, 2, tensor_part
    )
    chosen = jnp.where(kept_mask[:, :, None], chosen, jnp.zeros((), jnp.float32))
    token_grad = jnp.sum(chosen, axis=1).astype(jnp.bfloat16)
    hidden_part = gate_matrix.shape[1]
    width_share = model_width // lax.axis_size("dp")
    token_cols, grad_cols = (
        lax.all_to_all(routed, "dp", split_axis=1, concat_axis=0, tiled=True),
        lax.all_to_all(scaled, "dp", split_axis=1, concat_axis=0, tiled=True),
    )
    rows_each = routed.shape[0]

    def rounded_sum(left, right, form):
        product = jnp.einsum(form, left, right, preferred_element_type=jnp.float32)
        return jnp.sum(
            lax.optimization_barrier(product.astype(jnp.bfloat16)).astype(jnp.float32), axis=0
        )

    piece_gate = lax.all_gather(gate_delta, "dp", axis=0, tiled=True)
    piece_up = lax.all_gather(up_delta, "dp", axis=0, tiled=True)
    piece_hidden = lax.all_gather(hidden, "dp", axis=0, tiled=True)
    length = piece_gate.shape[0]
    groups = length // rows_each
    token_rows = token_cols.reshape(groups, rows_each, width_share)
    grad_rows = grad_cols.reshape(groups, rows_each, width_share)
    gate_rows = piece_gate.reshape(groups, rows_each, hidden_part)
    up_rows = piece_up.reshape(groups, rows_each, hidden_part)
    hidden_rows = piece_hidden.reshape(groups, rows_each, hidden_part)
    gate_sum = rounded_sum(token_rows, gate_rows, "nrk,nrf->nkf")
    up_sum = rounded_sum(token_rows, up_rows, "nrk,nrf->nkf")
    down_sum = rounded_sum(hidden_rows, grad_rows, "nrf,nrk->nfk")
    gate_grad = gate_sum.astype(jnp.bfloat16)
    up_grad = up_sum.astype(jnp.bfloat16)
    down_grad = down_sum.astype(jnp.bfloat16)
    return (token_grad, gate_grad[None], up_grad[None], down_grad[None])


def solution(mesh):
    return jax.shard_map(
        on_device,
        mesh=mesh,
        in_specs=(
            P(("expert", "dp"), None),
            P(("expert", "dp"), None),
            P(("expert", "dp"), None),
            P(("expert", "dp"), None),
            P(("expert", "dp"), None),
            P("expert", None, "tensor"),
            P("expert", None, "tensor"),
            P("expert", "tensor", None),
        ),
        out_specs=(
            P(("expert", "dp"), "tensor"),
            P("expert", "dp", "tensor"),
            P("expert", "dp", "tensor"),
            P("expert", "tensor", "dp"),
        ),
        check_vma=False,
    )
```

profile of v0, /device:TPU:0, one launch (start us, length us, event | category | flops | bytes accessed | tf_op | source)
XLA Modules:
  0.0 195.4 jit_solution(6368871402580833349)
XLA Ops:
  8.4 1.4 scatter_custom_fusion.1
  9.9 2.7 %gather_fusion.2 = bf16[192,4096]{1,0:T(8,128)(2,1)} fusion(bf16[128,4096]{1,0:T(8,128)(2,1)S(1)} %copy-done, s32[1024]{0:T(1024)S(1)} %pad_clamp_fusion.1), kind=kCustom, calls=%fused_computation.1.clone | custom fusion | bytes 3146496 | tf_op jit(solution)/shard_map/jit(_take)/gather | solution.py:27
  12.6 1.2 dynamic-slice_select_fusion
  13.8 17.9 %all_to_all.61 = bf16[4,48,1024]{2,1,0:T(8,128)(2,1)} all-to-all(bf16[4,48,1024]{2,1,0:T(8,128)(2,1)S(1)} %bitcast.73), channel_id=1, replica_groups=mesh['expert'=4,'dp'=2,'tensor'=4] {'expert'}, dimensions={0} | all-to-all | bytes 786432 | tf_op jit(solution)/shard_map/all_to_all | solution.py:36
  32.1 2.7 %gather_fusion.1 = bf16[192,4096]{1,0:T(8,128)(2,1)} fusion(bf16[128,4096]{1,0:T(8,128)(2,1)S(1)} %copy-done.1, s32[1024]{0:T(1024)S(1)} %pad_clamp_fusion.1), kind=kCustom, calls=%fused_computation.clone | custom fusion | bytes 3146496 | tf_op jit(solution)/shard_map/jit(_take)/gather | solution.py:29
  34.7 1.4 scatter_custom_fusion
  36.1 1.2 multiply_convert_fusion
  37.3 13.9 %all_to_all.62 = bf16[4,48,1024]{2,1,0:T(8,128)(2,1)} all-to-all(bf16[4,48,1024]{2,1,0:T(8,128)(2,1)S(1)} %bitcast.71), channel_id=1, replica_groups=mesh['expert'=4,'dp'=2,'tensor'=4] {'expert'}, dimensions={0} | all-to-all | bytes 786432 | tf_op jit(solution)/shard_map/all_to_all | solution.py:37
  51.3 3.6 %fusion.3 = f32[192,512]{1,0:T(8,128)S(1)} fusion(bf16[192,4096]{1,0:T(8,128)(2,1)} %all-gather.5.cloned.1.call-done, bf16[1,4096,512]{2,1,0:T(8,128)(2,1)} %param.15), kind=kOutput, calls=%fused_computation.9 | convolution fusion | flops 805306368 | bytes 6160384 | tf_op jit(solution)/shard_map/dot_general | solution.py:47
  55.0 16.9 %all-gather.3.cloned.1.call-done = bf16[192,4096]{1,0:T(8,128)(2,1)} async-done(((bf16[192,1024]{1,0:T(8,128)(2,1)}), bf16[192,4096]{1,0:T(8,128)(2,1)}) %all-gather.3.cloned.1.call-update) | async-done | bytes 1572880 | tf_op jit(solution)/shard_map/all_gather | solution.py:41
  71.9 4.3 %fusion.8 = f32[192,512]{1,0:T(8,128)S(1)} fusion(bf16[192,4096]{1,0:T(8,128)(2,1)} %all-gather.3.cloned.1.call-done, bf16[1,512,4096]{2,1,0:T(8,128)(2,1)} %param.17), kind=kOutput, calls=%fused_computation.14 | convolution fusion | flops 805306368 | bytes 6160384 | tf_op jit(solution)/shard_map/dot_general | solution.py:52
  76.3 1.8 multiply_convert_fusion.1
  78.5 1.5 fusion.1
  80.1 3.1 %fusion = f32[4096,192]{0,1:T(8,128)} fusion(f32[192,4096]{1,0:T(8,128)S(1)} %fusion.1, bf16[192,512]{1,0:T(8,128)(2,1)S(1)} %get-tuple-element.9, bf16[1,4096,512]{2,1,0:T(8,128)(2,1)S(1)} %copy-done.4), kind=kOutput, calls=%fused_computation.6 | convolution fusion | flops 806092800 | bytes 10682368 | tf_op jit(solution)/shard_map/dot_general | solution.py:66
  83.3 2.7 %copy.25 = bf16[24,2,8,2048]{3,2,0,1:T(8,128)(2,1)} copy(bf16[24,2,8,2048]{3,2,1,0:T(8,128)(2,1)} %bitcast.66) | data formatting | bytes 3145728 | tf_op jit(solution)/shard_map/all_to_all | solution.py:89
  86.0 4.8 %all-to-all-start.4 = ((bf16[192,2,2048]{2,0,1:T(8,128)(2,1)}), bf16[192,2,2048]{2,0,1:T(8,128)(2,1)}, u32[]{:S(2)}, u32[]{:S(2)}) async-start(bf16[192,2,2048]{2,0,1:T(8,128)(2,1)} %bitcast.55), calls=%async_computation.5 | async-start | bytes 3145728 | tf_op jit(solution)/shard_map/all_to_all | solution.py:89
  90.8 1.2 copy.26
  92.1 18.7 %all-to-all-done.4 = bf16[192,2,2048]{2,0,1:T(8,128)(2,1)} async-done(((bf16[192,2,2048]{2,0,1:T(8,128)(2,1)}), bf16[192,2,2048]{2,0,1:T(8,128)(2,1)}, u32[]{:S(2)}, u32[]{:S(2)}) %all-to-all-start.4) | async-done | bytes 1572896 | tf_op jit(solution)/shard_map/all_to_all | solution.py:89
  110.8 3.7 %all-to-all-start.3 = ((bf16[192,2,2048]{2,0,1:T(8,128)(2,1)}), bf16[192,2,2048]{2,0,1:T(8,128)(2,1)S(1)}, u32[]{:S(2)}, u32[]{:S(2)}) async-start(bf16[192,2,2048]{2,0,1:T(8,128)(2,1)} %bitcast.61), calls=%async_computation.4 | async-start | bytes 3145728 | tf_op jit(solution)/shard_map/all_to_all | solution.py:88
  115.0 22.7 %all_gather.17 = bf16[384,512]{1,0:T(8,128)(2,1)} all-gather(bf16[192,512]{1,0:T(8,128)(2,1)S(1)} %copy-done.7), channel_id=1, replica_groups=mesh['expert'=4,'dp'=2,'tensor'=4] {'dp'}, dimensions={0}, use_global_device_ids=true | all-gather | bytes 589824 | tf_op jit(solution)/shard_map/all_gather | solution.py:99
  137.8 6.4 %all_gather.18 = bf16[384,512]{1,0:T(8,128)(2,1)} all-gather(bf16[192,512]{1,0:T(8,128)(2,1)S(1)} %copy-done.9), channel_id=1, replica_groups=mesh['expert'=4,'dp'=2,'tensor'=4] {'dp'}, dimensions={0}, use_global_device_ids=true | all-gather | bytes 589824 | tf_op jit(solution)/shard_map/all_gather | solution.py:100
  144.2 4.6 %all-to-all-start.2 = ((f32[1024,4,48]{0,2,1:T(8,128)}), f32[1024,4,48]{0,2,1:T(8,128)S(1)}, u32[]{:S(2)}, u32[]{:S(2)}) async-start(f32[1024,4,48]{0,2,1:T(8,128)} %bitcast.74), calls=%async_computation.3 | async-start | bytes 1572864 | tf_op jit(solution)/shard_map/all_to_all | solution.py:71
  148.8 6.7 %all_gather.19 = bf16[384,512]{1,0:T(8,128)(2,1)S(1)} all-gather(bf16[192,512]{1,0:T(8,128)(2,1)} %get-tuple-element.7), channel_id=1, replica_groups=mesh['expert'=4,'dp'=2,'tensor'=4] {'dp'}, dimensions={0}, use_global_device_ids=true | all-gather | bytes 589824 | tf_op jit(solution)/shard_map/all_gather | solution.py:101
  155.5 4.7 %convolution_convert_fusion = bf16[2,512,2048]{2,1,0:T(8,128)(2,1)} fusion(bf16[2,192,512]{2,1,0:T(8,128)(2,1)S(1)} %bitcast.72, bf16[192,2,2048]{2,0,1:T(8,128)(2,1)} %all-to-all-done.4), kind=kOutput, calls=%fused_computation.16 | convolution fusion | flops 807403520 | bytes 6160384 | tf_op jit(solution)/shard_map/nrf,nrk->nfk/dot_general | solution.py:94
  160.2 3.4 %convolution_convert_fusion.1 = bf16[2,2048,512]{2,1,0:T(8,128)(2,1)} fusion(bf16[2,192,512]{2,1,0:T(8,128)(2,1)S(1)} %bitcast.69, bf16[192,2,2048]{2,0,1:T(8,128)(2,1)S(1)} %all-to-all-done.3), kind=kOutput, calls=%fused_computation.17 | convolution fusion | flops 807403520 | bytes 6160384 | tf_op jit(solution)/shard_map/nrk,nrf->nkf/dot_general | solution.py:94
  163.6 5.1 %reduce_sum.48 = bf16[512,2048]{1,0:T(8,128)(2,1)} reduce(bf16[2,512,2048]{2,1,0:T(8,128)(2,1)} %convolution_convert_fusion, bf16[]{:T(256)} %constant.52.clone.1), dimensions={0}, to_apply=%region_6.8 | reduce | flops 1048576 | bytes 6291458 | tf_op jit(solution)/shard_map/reduce_sum | solution.py:95
  168.6 4.9 %reduce_sum.47 = bf16[2048,512]{1,0:T(8,128)(2,1)} reduce(bf16[2,2048,512]{2,1,0:T(8,128)(2,1)} %convolution_convert_fusion.1, bf16[]{:T(256)} %constant.52.clone.1), dimensions={0}, to_apply=%region_5.7 | reduce | flops 1048576 | bytes 6291458 | tf_op jit(solution)/shard_map/reduce_sum | solution.py:95
  173.5 4.3 %convolution_convert_fusion.2 = bf16[2,2048,512]{2,1,0:T(8,128)(2,1)} fusion(bf16[2,192,512]{2,1,0:T(8,128)(2,1)} %bitcast.68, bf16[192,2,2048]{2,0,1:T(8,128)(2,1)S(1)} %all-to-all-done.3), kind=kOutput, calls=%fused_computation.18 | convolution fusion | flops 807403520 | bytes 6160384 | tf_op jit(solution)/shard_map/nrk,nrf->nkf/dot_general | solution.py:94
  177.9 4.9 %reduce_sum.46 = bf16[2048,512]{1,0:T(8,128)(2,1)} reduce(bf16[2,2048,512]{2,1,0:T(8,128)(2,1)} %convolution_convert_fusion.2, bf16[]{:T(256)} %constant.52.clone.1), dimensions={0}, to_apply=%region_4.6 | reduce | flops 1048576 | bytes 6291458 | tf_op jit(solution)/shard_map/reduce_sum | solution.py:95
  182.8 1.1 gather_fusion
  183.8 1.6 gather.10
  185.4 3.5 %select_reduce_fusion = bf16[128,1024]{1,0:T(8,128)(2,1)} fusion(f32[128,2,1024]{2,1,0:T(2,128)} %gather.10, pred[128,2]{1,0:T(8,128)(4,1)S(1)} %copy.15, pred[128,2]{1,0:T(8,128)(4,1)S(1)} %copy.14), kind=kLoop, calls=%fused_computation.24 | loop fusion | flops 655360 | bytes 1311232 | tf_op jit(solution)/shard_map/reduce_sum | solution.py:84
  (50 shorter events, 2.7 us)
Async XLA Ops:
  7.2 2.7 %copy-start = (bf16[128,4096]{1,0:T(8,128)(2,1)S(1)}, bf16[128,4096]{1,0:T(8,128)(2,1)}, u32[]{:S(2)}) copy-start(bf16[128,4096]{1,0:T(8,128)(2,1)} %param.10) | copy-start | bytes 3145732
  7.2 44.2 %all-gather.5.cloned.1.call-start = ((), (), s32[]{:S(2)}) async-start(), calls=%async_computation.7 | async-start | bytes 1966080 | tf_op jit(solution)/shard_map/all_gather | solution.py:40
  9.9 21.9 %copy-start.10 = (f32[128,2]{0,1:T(2,128)S(1)}, f32[128,2]{0,1:T(2,128)}, u32[]{:S(2)}) copy-start(f32[128,2]{0,1:T(2,128)} %param.14) | copy-start | bytes 3076
  12.6 19.5 %copy-start.1 = (bf16[128,4096]{1,0:T(8,128)(2,1)S(1)}, bf16[128,4096]{1,0:T(8,128)(2,1)}, u32[]{:S(2)}) copy-start(bf16[128,4096]{1,0:T(8,128)(2,1)} %param.11) | copy-start | bytes 3145732
  31.7 40.2 %all-gather.3.cloned.1.call-start = ((), (), s32[]{:S(2)}) async-start(), calls=%async_computation.6 | async-start | bytes 1966080 | tf_op jit(solution)/shard_map/all_gather | solution.py:41
  51.3 92.9 %reduce-scatter.2.cloned.1.call-start = ((), (), s32[]{:S(2)}) async-start(), calls=%async_computation.8 | async-start | bytes 3932160 | tf_op jit(solution)/shard_map/reduce_scatter | solution.py:64
  55.0 21.3 %copy-start.3 = (bf16[192,4096]{1,0:T(8,128)(2,1)S(1)}, bf16[192,4096]{1,0:T(8,128)(2,1)}, u32[]{:S(2)}) copy-start(bf16[192,4096]{1,0:T(8,128)(2,1)} %all-gather.5.cloned.1.call-done) | copy-start | bytes 4718596
  71.9 4.4 %copy-start.4 = (bf16[1,4096,512]{2,1,0:T(8,128)(2,1)S(1)}, bf16[1,4096,512]{2,1,0:T(8,128)(2,1)}, u32[]{:S(2)}) copy-start(bf16[1,4096,512]{2,1,0:T(8,128)(2,1)} %param.16) | copy-start | bytes 12582916
  76.3 2.3 %copy-start.2 = (bf16[1,4096,512]{2,1,0:T(8,128)(2,1)S(1)}, bf16[1,4096,512]{2,1,0:T(8,128)(2,1)}, u32[]{:S(2)}) copy-start(bf16[1,4096,512]{2,1,0:T(8,128)(2,1)} %param.15) | copy-start | bytes 12582916
  78.1 2.0 %copy-start.6 = (bf16[192,512]{1,0:T(8,128)(2,1)}, bf16[192,512]{1,0:T(8,128)(2,1)S(1)}, u32[]{:S(2)}) copy-start(bf16[192,512]{1,0:T(8,128)(2,1)S(1)} %get-tuple-element.8) | copy-start | bytes 589828
  78.1 2.0 %copy-start.8 = (bf16[192,512]{1,0:T(8,128)(2,1)}, bf16[192,512]{1,0:T(8,128)(2,1)S(1)}, u32[]{:S(2)}) copy-start(bf16[192,512]{1,0:T(8,128)(2,1)S(1)} %get-tuple-element.9) | copy-start | bytes 589828
  86.0 24.8 %all-to-all-start.4 = ((bf16[192,2,2048]{2,0,1:T(8,128)(2,1)}), bf16[192,2,2048]{2,0,1:T(8,128)(2,1)}, u32[]{:S(2)}, u32[]{:S(2)}) async-start(bf16[192,2,2048]{2,0,1:T(8,128)(2,1)} %bitcast.55), calls=%async_computation.5 | async-start | bytes 3145728 | tf_op jit(solution)/shard_map/all_to_all | solution.py:89
  92.1 22.9 %copy-start.7 = (bf16[192,512]{1,0:T(8,128)(2,1)S(1)}, bf16[192,512]{1,0:T(8,128)(2,1)}, u32[]{:S(2)}) copy-start(bf16[192,512]{1,0:T(8,128)(2,1)} %copy-done.6) | copy-start | bytes 589828
  92.1 45.7 %copy-start.9 = (bf16[192,512]{1,0:T(8,128)(2,1)S(1)}, bf16[192,512]{1,0:T(8,128)(2,1)}, u32[]{:S(2)}) copy-start(bf16[192,512]{1,0:T(8,128)(2,1)} %copy-done.8) | copy-start | bytes 589828
  110.8 33.5 %all-to-all-start.3 = ((bf16[192,2,2048]{2,0,1:T(8,128)(2,1)}), bf16[192,2,2048]{2,0,1:T(8,128)(2,1)S(1)}, u32[]{:S(2)}, u32[]{:S(2)}) async-start(bf16[192,2,2048]{2,0,1:T(8,128)(2,1)} %bitcast.61), calls=%async_computation.4 | async-start | bytes 3145728 | tf_op jit(solution)/shard_map/all_to_all | solution.py:88
  144.2 38.5 %all-to-all-start.2 = ((f32[1024,4,48]{0,2,1:T(8,128)}), f32[1024,4,48]{0,2,1:T(8,128)S(1)}, u32[]{:S(2)}, u32[]{:S(2)}) async-start(f32[1024,4,48]{0,2,1:T(8,128)} %bitcast.74), calls=%async_computation.3 | async-start | bytes 1572864 | tf_op jit(solution)/shard_map/all_to_all | solution.py:71
  155.5 4.7 %copy-start.5 = (bf16[384,512]{1,0:T(8,128)(2,1)S(1)}, bf16[384,512]{1,0:T(8,128)(2,1)}, u32[]{:S(2)}) copy-start(bf16[384,512]{1,0:T(8,128)(2,1)} %all_gather.18) | copy-start | bytes 1179652
Sparse Core Ops, SparseCore 0:
  31.9 18.7 all-gather.4
  52.2 19.6 all-gather.2
  83.4 37.9 reduce-scatter.1
where the time goes:
time: 196 us; the launch traced here: 195 us
  blocking collectives  67.7 us (35%)
  waiting for transfers between devices  35.6 us (18%)
  matrix products  26.8 us (14%)
  other arithmetic  21.6 us (11%)
  local copies, waits for them, and re-layouts  16.4 us (8%)
  between operations  14 us (7%)
  starting transfers between devices  13.2 us (7%)
    all_gather x1, blocking collectives, on_device(): piece_gate = lax.all_gather(gate_delta, 'dp', axis=0, tiled=True)  22.7 us
    all_to_all x1, waiting for transfers between devices, on_device(): lax.all_to_all(scaled, 'dp', split_axis=1, concat_axis=0, tiled=True)  18.7 us
    all_to_all x1, blocking collectives, on_device(): lax.all_to_all(token_share, 'expert', split_axis=0, concat_axis=0, tiled=...  17.9 us
    all_gather x1, waiting for transfers between devices, on_device(): lax.all_gather(grad_share, 'tensor', axis=1, tiled=True)  16.9 us
    reduce_sum x3, other arithmetic, rounded_sum(): jnp.sum(lax.optimization_barrier(product.astype(jnp.bfloat16)).astype(jnp...  14.9 us
    all_to_all x1, blocking collectives, on_device(): lax.all_to_all(grad_share, 'expert', split_axis=0, concat_axis=0, tiled=T...  13.9 us
    dot_general x3, matrix products, rounded_sum(): product = jnp.einsum(form, left, right, preferred_element_type=jnp.float32)  12.4 us
    all_gather x1, blocking collectives, on_device(): piece_hidden = lax.all_gather(hidden, 'dp', axis=0, tiled=True)  6.73 us
  transfers between devices with their start and end apart: 6, of which 2 were waited for; matrix products, arithmetic and copies ran while one was open for 21% of the time, Pallas kernels for 0%

commit v1 on v0

--- a/solution.py
+++ b/solution.py
@@ -1,7 +1,346 @@
+import functools
+
 import jax
 import jax.numpy as jnp
 from jax import lax
+from jax.experimental import pallas as pl
+from jax.experimental.pallas import tpu as pltpu
 from jax.sharding import PartitionSpec as P
+
+MESH = pl.DeviceIdType.MESH
+LAST = (((1,), (1,)), ((), ()))
+FIRST = (((0,), (0,)), ((), ()))
+
+
+def greet(sizes):
+    experts = sizes
+    e = lax.axis_index("expert")
+    g = lax.axis_index("dp")
+    t = lax.axis_index("tensor")
+    sib = t + 1 - 2 * lax.rem(t, 2)
+    opp = lax.rem(t + 2, 4)
+    barrier = pltpu.get_barrier_semaphore()
+    partners = [(e, g, sib), (e, g, opp), (e, 1 - g, t)]
+    partners += [(lax.rem(e + d, experts), g, t) for d in range(1, experts)]
+    for who in partners:
+        pl.semaphore_signal(barrier, inc=1, device_id=who, device_id_type=MESH)
+    return e, g, t, partners, barrier
+
+
+def one_hot(ei, si, k, capacity, slots):
+    exp = ei[:, k : k + 1]
+    slot = si[:, k : k + 1]
+    target = jnp.where(slot < capacity, exp * capacity + slot, slots)
+    place = lax.broadcasted_iota(jnp.int32, (ei.shape[0], slots), 1)
+    return jnp.where(place == target, 1.0, 0.0).astype(jnp.bfloat16)
+
+
+def dispatch_kernel(
+    experts, tok, grd, ei, si, prob, got, oth, send,
+    z_s, z_r, x_s, x_r, b_s, b_r, y_s, y_r, o_s, o_r
+):
+    e, g, t, partners, barrier = greet(experts)
+    sib, opp, other = partners[:3]
+    slots, width = send.shape[2], send.shape[3]
+    half = tok.shape[1] // 2
+    capacity = slots // experts
+
+    first = one_hot(ei[...], si[...], 0, capacity, slots)
+    second = one_hot(ei[...], si[...], 1, capacity, slots)
+    both = first + second
+    for h in range(2):
+        cols = pl.ds(pl.multiple_of(h * half + t * width, width), width)
+        send[0, h] = lax.dot_general(
+            both, tok[:, cols], FIRST, preferred_element_type=jnp.float32
+        ).astype(jnp.bfloat16)
+        cot = grd[:, cols].astype(jnp.float32)
+        send[1, h] = (
+            lax.dot_general(
+                first, (prob[:, 0:1] * cot).astype(jnp.bfloat16), FIRST,
+                preferred_element_type=jnp.float32,
+            )
+            + lax.dot_general(
+                second, (prob[:, 1:2] * cot).astype(jnp.bfloat16), FIRST,
+                preferred_element_type=jnp.float32,
+            )
+        ).astype(jnp.bfloat16)
+    pl.semaphore_wait(barrier, len(partners))
+
+    def rows(s):
+        return pl.ds(pl.multiple_of(s * capacity, 16), capacity)
+
+    def window(q):
+        return pl.ds(pl.multiple_of(q * width, width), width)
+
+    mine, across = window(t), window(opp[2])
+    sends, recvs = [], []
+
+    def remote(src, dst, s_sem, r_sem, who):
+        copy = pltpu.make_async_remote_copy(
+            src_ref=src, dst_ref=dst, send_sem=s_sem, recv_sem=r_sem,
+            device_id=who, device_id_type=MESH,
+        )
+        copy.start()
+        sends.append(copy)
+        return copy
+
+    z, x = {}, {}
+    for a in range(2):
+        for d in (2, 3, 1):
+            if d < experts:
+                z[d, a] = remote(
+                    send.at[a, :, rows(lax.rem(e + d, experts))],
+                    got.at[a, :, rows(e), mine],
+                    z_s.at[d, a], z_r.at[d, a], partners[2 + d],
+                )
+    for a in range(2):
+        for h in range(2):
+            got[a, h, rows(e), mine] = send[a, h, rows(e)]
+    for d in (0, 1, 3, 2):
+        block = rows(lax.rem(e + experts - d, experts))
+        for a in range(2):
+            if d:
+                z[d, a].wait_recv()
+            here = got.at[a, :, block, mine]
+            x[d, a] = remote(here, here, x_s.at[d, a], x_r.at[d, a], opp)
+            recvs.append(remote(here, here, b_s.at[d, a, 0], b_r.at[d, a, 0], sib))
+    y = {}
+    for a in range(2):
+        y[a, 0] = remote(
+            got.at[a, 1 - g, :, mine], oth.at[a, :, mine],
+            y_s.at[a, 0], y_r.at[a, 0], other,
+        )
+    for d in (0, 1, 3, 2):
+        block = rows(lax.rem(e + experts - d, experts))
+        for a in range(2):
+            x[d, a].wait_recv()
+            here = got.at[a, :, block, across]
+            recvs.append(remote(here, here, b_s.at[d, a, 1], b_r.at[d, a, 1], sib))
+    for a in range(2):
+        y[a, 1] = remote(
+            got.at[a, 1 - g, :, across], oth.at[a, :, across],
+            y_s.at[a, 1], y_r.at[a, 1], other,
+        )
+    for i in range(2):
+        for a in range(2):
+            y[a, i].wait_recv()
+            here = oth.at[a, :, across if i else mine]
+            recvs.append(remote(here, here, o_s.at[a, i], o_r.at[a, i], sib))
+    for copy in recvs:
+        copy.wait_recv()
+    for copy in sends:
+        copy.wait_send()
+
+
+def return_kernel(
+    experts, delta, wg, wu, ei, si, out, oth, part, near, far_out, far, total, back,
+    y_s, y_r, b_s, b_r, x_s, x_r, z_s, z_r
+):
+    e, g, t, partners, barrier = greet(experts)
+    sib, opp, other = partners[:3]
+    slots, width = back.shape
+    capacity = slots // experts
+    tile = 512
+    c = lax.rem(t, 2)
+    xi = t // 2
+    sends = []
+
+    def remote(src, dst, s_sem, r_sem, who):
+        copy = pltpu.make_async_remote_copy(
+            src_ref=src, dst_ref=dst, send_sem=s_sem, recv_sem=r_sem,
+            device_id=who, device_id_type=MESH,
+        )
+        copy.start()
+        sends.append(copy)
+        return copy
+
+    def product(q):
+        @pl.loop(0, width // tile)
+        def _(i):
+            block = pl.ds(pl.multiple_of(q * width + i * tile, tile), tile)
+            value = lax.dot_general(
+                delta[0], wg[block, :], LAST, preferred_element_type=jnp.float32
+            ) + lax.dot_general(
+                delta[1], wu[block, :], LAST, preferred_element_type=jnp.float32
+            )
+            part[q, :, pl.ds(pl.multiple_of(i * tile, tile), tile)] = value.astype(jnp.bfloat16)
+
+    def rows(s):
+        return pl.ds(pl.multiple_of(s * capacity, 16), capacity)
+
+    pl.semaphore_wait(barrier, len(partners))
+    y = [
+        remote(delta.at[k], oth.at[k], y_s.at[k], y_r.at[k], other) for k in range(3)
+    ]
+    q_far, q_near = (1 - xi) * 2, xi * 2
+    product(q_far + 1 - c)
+    b_far = remote(part.at[q_far + 1 - c], near.at[0], b_s.at[0], b_r.at[0], sib)
+    product(q_far + c)
+    b_far.wait_recv()
+    order = (2, 3, 1, 0)
+    x = {}
+    for d in order:
+        block = rows(lax.rem(e + d, experts))
+        far_out[block] = (
+            part[q_far + c, block].astype(jnp.float32) + near[0, block].astype(jnp.float32)
+        ).astype(jnp.bfloat16)
+        x[d] = remote(far_out.at[block], far.at[block], x_s.at[d], x_r.at[d], opp)
+    product(q_near + 1 - c)
+    b_near = remote(part.at[q_near + 1 - c], near.at[1], b_s.at[1], b_r.at[1], sib)
+    product(q_near + c)
+    b_near.wait_recv()
+    z = {}
+    for d in order:
+        who = lax.rem(e + d, experts)
+        block = rows(who)
+        x[d].wait_recv()
+        value = (
+            part[q_near + c, block].astype(jnp.float32)
+            + near[1, block].astype(jnp.float32)
+            + far[block].astype(jnp.float32)
+        ).astype(jnp.bfloat16)
+        if d:
+            total[block] = value
+            z[d] = remote(total.at[block], back.at[rows(e)], z_s.at[d], z_r.at[d], partners[2 + d])
+        else:
+            back[block] = value
+    pick = one_hot(ei[...], si[...], 0, capacity, slots) + one_hot(
+        ei[...], si[...], 1, capacity, slots
+    )
+    for d in (1, 3, 2):
+        z[d].wait_recv()
+    out[...] = jnp.dot(pick, back[...], preferred_element_type=jnp.float32).astype(jnp.bfloat16)
+    for copy in y:
+        copy.wait_recv()
+    for copy in sends:
+        copy.wait_send()
+
+
+VMEM = pl.BlockSpec(memory_space=pltpu.VMEM)
+DMA = pltpu.SemaphoreType.DMA
+
+
+def params(identity):
+    return pltpu.CompilerParams(
+        collective_id=identity, has_side_effects=True, vmem_limit_bytes=48 * 1024 * 1024
+    )
+
+
+def fast_on_device(
+    tokens, out_grad, expert_index, slot_index, gate_probs, gate_weight, up_weight, down_weight
+):
+    local_rows, model_width = tokens.shape
+    experts = lax.axis_size("expert")
+    slots = 3 * local_rows // 2
+    hidden_part = gate_weight.shape[2]
+    half = model_width // 2
+    width = half // lax.axis_size("tensor")
+    share = model_width // lax.axis_size("tensor")
+    bf = jnp.bfloat16
+    got, oth = pl.pallas_call(
+        functools.partial(dispatch_kernel, experts),
+        out_shape=(
+            jax.ShapeDtypeStruct((2, 2, slots, half), bf),
+            jax.ShapeDtypeStruct((2, slots, half), bf),
+        ),
+        in_specs=[VMEM] * 5,
+        out_specs=(VMEM, VMEM),
+        scratch_shapes=[
+            pltpu.VMEM((2, 2, slots, width), bf),
+            DMA((experts, 2)), DMA((experts, 2)),
+            DMA((experts, 2)), DMA((experts, 2)),
+            DMA((experts, 2, 2)), DMA((experts, 2, 2)),
+            DMA((2, 2)), DMA((2, 2)),
+            DMA((2, 2)), DMA((2, 2)),
+        ],
+        compiler_params=params(0),
+        name="dispatch",
+    )(tokens, out_grad, expert_index, slot_index, gate_probs)
+    gate_matrix, up_matrix, down_matrix = gate_weight[0], up_weight[0], down_weight[0]
+
+    def forward(rows, matrix):
+        return sum(
+            jnp.dot(rows[h], matrix[h * half : (h + 1) * half], preferred_element_type=jnp.float32)
+            for h in range(2)
+        )
+
+    gate_value = forward(got[0], gate_matrix)
+    up_value = forward(got[0], up_matrix)
+    back_grad = sum(
+        lax.dot_general(
+            got[1, h], down_matrix[:, h * half : (h + 1) * half], LAST,
+            preferred_element_type=jnp.float32,
+        )
+        for h in range(2)
+    )
+    gate_sigmoid = jax.nn.sigmoid(gate_value)
+    activated = gate_value * gate_sigmoid
+    hidden = (activated * up_value).astype(bf)
+    gate_delta = (
+        back_grad * up_value * gate_sigmoid * (1.0 + gate_value * (1.0 - gate_sigmoid))
+    ).astype(bf)
+    up_delta = (back_grad * activated).astype(bf)
+    delta = jnp.stack([gate_delta, up_delta, hidden])
+    token_grad, delta_oth = pl.pallas_call(
+        functools.partial(return_kernel, experts),
+        out_shape=(
+            jax.ShapeDtypeStruct((local_rows, share), bf),
+            jax.ShapeDtypeStruct((3, slots, hidden_part), bf),
+        ),
+        in_specs=[VMEM] * 5,
+        out_specs=(VMEM, VMEM),
+        scratch_shapes=[
+            pltpu.VMEM((4, slots, share), bf),
+            pltpu.VMEM((2, slots, share), bf),
+            pltpu.VMEM((slots, share), bf),
+            pltpu.VMEM((slots, share), bf),
+            pltpu.VMEM((slots, share), bf),
+            pltpu.VMEM((slots, share), bf),
+            DMA((3,)), DMA((3,)),
+            DMA((2,)), DMA((2,)),
+            DMA((experts,)), DMA((experts,)),
+            DMA((experts,)), DMA((experts,)),
+        ],
+        compiler_params=params(1),
+        name="giveback",
+    )(delta, gate_matrix, up_matrix, expert_index, slot_index)
+
+    def grads_kernel(got_ref, oth_ref, delta_ref, delta_oth_ref, gg, ug, dg):
+        g = lax.axis_index("dp")
+        i = pl.program_id(0)
+        n = gg.shape[0]
+        cols = pl.ds(pl.multiple_of(i * n, n), n)
+
+        def both(a_own, a_oth, b_own, b_oth):
+            return (
+                lax.dot_general(a_own, b_own, FIRST, preferred_element_type=jnp.float32)
+                + lax.dot_general(a_oth, b_oth, FIRST, preferred_element_type=jnp.float32)
+            ).astype(bf)
+
+        tok_own, tok_oth = got_ref[0, g, :, cols], oth_ref[0, :, cols]
+        gg[...] = both(tok_own, tok_oth, delta_ref[0], delta_oth_ref[0])
+        ug[...] = both(tok_own, tok_oth, delta_ref[1], delta_oth_ref[1])
+        dg[...] = both(delta_ref[2], delta_oth_ref[2], got_ref[1, g, :, cols], oth_ref[1, :, cols])
+
+    tile = 512
+    gate_grad, up_grad, down_grad = pl.pallas_call(
+        grads_kernel,
+        grid=(half // tile,),
+        out_shape=(
+            jax.ShapeDtypeStruct((half, hidden_part), bf),
+            jax.ShapeDtypeStruct((half, hidden_part), bf),
+            jax.ShapeDtypeStruct((hidden_part, half), bf),
+        ),
+        in_specs=[VMEM] * 4,
+        out_specs=(
+            pl.BlockSpec((tile, hidden_part), lambda i: (i, 0)),
+            pl.BlockSpec((tile, hidden_part), lambda i: (i, 0)),
+            pl.BlockSpec((hidden_part, tile), lambda i: (0, i)),
+        ),
+        compiler_params=pltpu.CompilerParams(vmem_limit_bytes=48 * 1024 * 1024),
+        name="weight_grads",
+    )(got, oth, delta, delta_oth)
+    return (token_grad, gate_grad[None], up_grad[None], down_grad[None])
 
 
 def on_device(
@@ -116,8 +455,23 @@
 
 
 def solution(mesh):
+    sizes = dict(mesh.shape)
+
+    def body(*args):
+        local_rows, model_width = args[0].shape
+        capacity = 3 * local_rows // (2 * sizes["expert"])
+        fits = (
+            sizes["expert"] == 4
+            and sizes["dp"] == 2
+            and sizes["tensor"] == 4
+            and capacity % 16 == 0
+            and model_width % 4096 == 0
+            and args[5].shape[2] % 256 == 0
+        )
+        return fast_on_device(*args) if fits else on_device(*args)
+
     return jax.shard_map(
-        on_device,
+        body,
         mesh=mesh,
         in_specs=(
             P(("expert", "dp"), None),

time: 196 us -> 90.4 us (0.46)
  Pallas kernels: 0 us -> 72.5 us
  blocking collectives: 67.7 us -> 0 us
  waiting for transfers between devices: 35.6 us -> 0 us
  other arithmetic: 21.6 us -> 0.07 us
  matrix products: 26.8 us -> 8.95 us
  between operations: 14 us -> 0.72 us
  starting transfers between devices: 13.2 us -> 0 us
  local copies, waits for them, and re-layouts: 16.4 us -> 7.86 us
    pallas_call x0 -> x3, Pallas kernels: none -> 72.5 us  [the longest x1 44.2 us: fast_on_device(): pl.pallas_call(functools.partial(dispatch_kernel, experts), out_shape=(ja...]
    all_gather x3 -> x0, blocking collectives: 35.9 us -> none  [the longest x1 22.7 us: on_device(): piece_gate = lax.all_gather(gate_delta, 'dp', axis=0, tiled=True)]
    all_to_all x2 -> x0, blocking collectives: 31.8 us -> none  [the longest x1 17.9 us: on_device(): lax.all_to_all(token_share, 'expert', split_axis=0, concat_axis=0, tiled=...]
    all_to_all x3 -> x0, waiting for transfers between devices: 18.7 us -> none  [the longest x1 18.7 us: on_device(): lax.all_to_all(scaled, 'dp', split_axis=1, concat_axis=0, tiled=True)]
    reduce_sum x4 -> x0, other arithmetic: 18.3 us -> none  [the longest x3 14.9 us: rounded_sum(): jnp.sum(lax.optimization_barrier(product.astype(jnp.bfloat16)).astype(jnp...]
    dot_general x8 -> x6, matrix products: 26.8 us -> 8.95 us  [the longest x4 7.16 us: forward(): jnp.dot(rows[h], matrix[h * half:(h + 1) * half], preferred_element_type=...]
    all_gather x2 -> x0, waiting for transfers between devices: 16.9 us -> none  [the longest x1 16.9 us: on_device(): lax.all_gather(grad_share, 'tensor', axis=1, tiled=True)]
    all_to_all x3 -> x0, starting transfers between devices: 13.1 us -> none  [the longest x1 4.83 us: on_device(): lax.all_to_all(scaled, 'dp', split_axis=1, concat_axis=0, tiled=True)]
  transfers between devices with their start and end apart: 6 -> 0, of which waited for: 2 -> 0; matrix products, arithmetic and copies ran while one was open for 21% -> 0% of each run, Pallas kernels for 0% -> 0%
where the time goes in v1:
time: 90.4 us; the launch traced here: 90.1 us
  Pallas kernels  72.5 us (80%)
  matrix products  8.95 us (10%)
  local copies, waits for them, and re-layouts  7.86 us (9%)
    pallas_call x1, Pallas kernels, fast_on_device(): pl.pallas_call(functools.partial(dispatch_kernel, experts), out_shape=(ja...  44.2 us
    pallas_call x1, Pallas kernels, fast_on_device(): pl.pallas_call(functools.partial(return_kernel, experts), out_shape=(jax....  23.3 us
    unnamed x16, local copies, waits for them, and re-layouts  7.86 us
    dot_general x4, matrix products, forward(): jnp.dot(rows[h], matrix[h * half:(h + 1) * half], preferred_element_type=...  7.16 us
    pallas_call x1, Pallas kernels, fast_on_device(): pl.pallas_call(grads_kernel, grid=(half // tile,), out_shape=(jax.ShapeDt...  5.02 us

profile of v1, /device:TPU:0, one launch (start us, length us, event | category | flops | bytes accessed | tf_op | source)
XLA Modules:
  0.0 90.1 jit_solution(5916773081836123177)
XLA Ops:
  0.6 0.8 copy.12.ei
  1.4 0.8 copy.13.si
  2.2 0.8 copy.14.prob
  3.0 0.0 copy-start.2
  3.0 1.2 %copy-done.2 = bf16[128,4096]{1,0:T(8,128)(2,1)S(1)} copy-done((bf16[128,4096]{1,0:T(8,128)(2,1)S(1)}, bf16[128,4096]{1,0:T(8,128)(2,1)}, u32[]{:S(2)}) %copy-start.2) | copy-done | bytes 1048600
  4.2 0.0 copy-start.3
  4.2 1.2 %copy-done.3 = bf16[128,4096]{1,0:T(8,128)(2,1)S(1)} copy-done((bf16[128,4096]{1,0:T(8,128)(2,1)S(1)}, bf16[128,4096]{1,0:T(8,128)(2,1)}, u32[]{:S(2)}) %copy-start.3) | copy-done | bytes 1048600
  5.4 0.0 copy-start
  5.4 44.2 %dispatch.1 = (bf16[2,2,192,2048]{3,2,1,0:T(8,128)(2,1)}, bf16[2,192,2048]{2,1,0:T(8,128)(2,1)S(1)}) custom-call(bf16[128,4096]{1,0:T(8,128)(2,1)S(1)} %copy-done.2, bf16[128,4096]{1,0:T(8,128)(2,1)S(1)} %copy-done.3, s32[128,2]{1,0:T(8,128)S(1)} %copy.12.ei, s32[128,2]{1,0:T(8,128)S(1)} %copy.13.si, f32[128,2]{1,0:T(8,128)S(1)} %copy.14.prob), custom_call_target="tpu_custom_call" | custom-call | tf_op jit(solution)/shard_map/dispatch/pallas_call | solution.py:240
  49.6 2.4 %fusion.4 = f32[192,512]{1,0:T(8,128)S(1)} fusion(bf16[1,4096,512]{2,1,0:T(8,128)(2,1)} %param.13, bf16[2,2,192,2048]{3,2,1,0:T(8,128)(2,1)} %get-tuple-element.11.got_ref), kind=kOutput, calls=%fused_computation.4 | convolution fusion | flops 402653184 | bytes 3276800 | tf_op jit(solution)/shard_map/dot_general | solution.py:263
  52.0 0.0 copy-done
  52.1 0.0 copy-start.1
  52.1 1.9 %fusion.19 = f32[192,512]{1,0:T(8,128)S(1)} fusion(f32[192,512]{1,0:T(8,128)S(1)} %fusion.4, bf16[1,4096,512]{2,1,0:T(8,128)(2,1)S(1)} %copy-done, bf16[2,2,192,2048]{3,2,1,0:T(8,128)(2,1)} %get-tuple-element.11.got_ref), kind=kOutput, calls=%fused_computation.17 | convolution fusion | flops 402751488 | bytes 3670016 | tf_op jit(solution)/shard_map/dot_general | solution.py:263
  53.9 0.2 copy-done.1
  54.2 0.0 copy-start.4
  54.2 2.3 %fusion.8 = f32[192,512]{1,0:T(8,128)S(1)} fusion(bf16[1,4096,512]{2,1,0:T(8,128)(2,1)} %param.14, bf16[2,2,192,2048]{3,2,1,0:T(8,128)(2,1)S(1)} %copy-done.1), kind=kOutput, calls=%fused_computation.8 | convolution fusion | flops 402653184 | bytes 3276800 | tf_op jit(solution)/shard_map/dot_general | solution.py:263
  56.5 0.5 copy-done.4
  57.0 0.0 copy-start.5
  57.0 0.6 fusion.16
  57.6 1.6 %copy-done.5 = bf16[1,512,4096]{2,1,0:T(8,128)(2,1)S(1)} copy-done((bf16[1,512,4096]{2,1,0:T(8,128)(2,1)S(1)}, bf16[1,512,4096]{2,1,0:T(8,128)(2,1)}, u32[]{:S(2)}) %copy-start.5) | copy-done | bytes 4194328
  59.2 0.8 fusion
  60.0 0.9 %fusion.40 = (bf16[1,192,512]{2,1,0:T(8,128)(2,1)S(1)}, bf16[1,192,512]{2,1,0:T(8,128)(2,1)S(1)}, bf16[1,192,512]{2,1,0:T(8,128)(2,1)S(1)}) fusion(f32[192,512]{1,0:T(8,128)S(1)} %fusion.19, f32[192,512]{1,0:T(8,128)S(1)} %fusion.16, f32[192,512]{1,0:T(8,128)S(1)} %fusion, bf16[512,4096]{1,0:T(8,128)(2,1)S(1)} %bitcast.49, ...), kind=kOutput, calls=%fused_computation.39 | convolution fusion | flops 404226048 | bytes 4653056 | tf_op jit(solution)/shard_map/dot_general | solution.py:270
  61.0 0.1 pad_maximum_fusion.delta.delta_ref
  61.1 23.3 %giveback.1 = (bf16[128,1024]{1,0:T(8,128)(2,1)S(1)}, bf16[3,192,512]{2,1,0:T(8,128)(2,1)S(1)}) custom-call(bf16[3,192,512]{2,1,0:T(8,128)(2,1)S(1)} %pad_maximum_fusion.delta.delta_ref, bf16[4096,512]{1,0:T(8,128)(2,1)S(1)} %bitcast.46, bf16[4096,512]{1,0:T(8,128)(2,1)} %bitcast.47, s32[128,2]{1,0:T(8,128)S(1)} %copy.12.ei, s32[128,2]{1,0:T(8,128)S(1)} %copy.13.si), custom_call_target="tpu_custom_call" | custom-call | tf_op jit(solution)/shard_map/giveback/pallas_call | solution.py:284
  84.4 5.0 %weight_grads.1 = (bf16[2048,512]{1,0:T(8,128)(2,1)}, bf16[2048,512]{1,0:T(8,128)(2,1)}, bf16[512,2048]{1,0:T(8,128)(2,1)}) custom-call(bf16[2,2,192,2048]{3,2,1,0:T(8,128)(2,1)S(1)} %copy-done.1, bf16[2,192,2048]{2,1,0:T(8,128)(2,1)S(1)} %get-tuple-element.13.oth_ref, bf16[3,192,512]{2,1,0:T(8,128)(2,1)S(1)} %pad_maximum_fusion.delta.delta_ref, ...), custom_call_target="tpu_custom_call" | custom-call | tf_op jit(solution)/shard_map/weight_grads/pallas_call | solution.py:326
  89.4 0.7 copy.18
Async XLA Ops:
  3.0 1.2 %copy-start.2 = (bf16[128,4096]{1,0:T(8,128)(2,1)S(1)}, bf16[128,4096]{1,0:T(8,128)(2,1)}, u32[]{:S(2)}) copy-start(bf16[128,4096]{1,0:T(8,128)(2,1)} %tok.1) | copy-start | bytes 3145732
  4.2 1.2 %copy-start.3 = (bf16[128,4096]{1,0:T(8,128)(2,1)S(1)}, bf16[128,4096]{1,0:T(8,128)(2,1)}, u32[]{:S(2)}) copy-start(bf16[128,4096]{1,0:T(8,128)(2,1)} %grd.1) | copy-start | bytes 3145732
  5.4 46.6 %copy-start = (bf16[1,4096,512]{2,1,0:T(8,128)(2,1)S(1)}, bf16[1,4096,512]{2,1,0:T(8,128)(2,1)}, u32[]{:S(2)}) copy-start(bf16[1,4096,512]{2,1,0:T(8,128)(2,1)} %param.13) | copy-start | bytes 12582916
  52.1 2.1 %copy-start.1 = (bf16[2,2,192,2048]{3,2,1,0:T(8,128)(2,1)S(1)}, bf16[2,2,192,2048]{3,2,1,0:T(8,128)(2,1)}, u32[]{:S(2)}) copy-start(bf16[2,2,192,2048]{3,2,1,0:T(8,128)(2,1)} %get-tuple-element.11.got_ref) | copy-start | bytes 9437188
  54.2 2.8 %copy-start.4 = (bf16[1,4096,512]{2,1,0:T(8,128)(2,1)S(1)}, bf16[1,4096,512]{2,1,0:T(8,128)(2,1)}, u32[]{:S(2)}) copy-start(bf16[1,4096,512]{2,1,0:T(8,128)(2,1)} %param.14) | copy-start | bytes 12582916
  57.0 2.2 %copy-start.5 = (bf16[1,512,4096]{2,1,0:T(8,128)(2,1)S(1)}, bf16[1,512,4096]{2,1,0:T(8,128)(2,1)}, u32[]{:S(2)}) copy-start(bf16[1,512,4096]{2,1,0:T(8,128)(2,1)} %param.15) | copy-start | bytes 12582916

commit v2 on v0

--- a/solution.py
+++ b/solution.py
@@ -1,7 +1,364 @@
+import functools
+
 import jax
 import jax.numpy as jnp
 from jax import lax
+from jax.experimental import pallas as pl
+from jax.experimental.pallas import tpu as pltpu
 from jax.sharding import PartitionSpec as P
+
+MESH = pl.DeviceIdType.MESH
+LAST = (((1,), (1,)), ((), ()))
+FIRST = (((0,), (0,)), ((), ()))
+
+
+def greet(sizes):
+    experts = sizes
+    e = lax.axis_index("expert")
+    g = lax.axis_index("dp")
+    t = lax.axis_index("tensor")
+    sib = t + 1 - 2 * lax.rem(t, 2)
+    opp = lax.rem(t + 2, 4)
+    barrier = pltpu.get_barrier_semaphore()
+    partners = [(e, g, sib), (e, g, opp), (e, 1 - g, t)]
+    partners += [(lax.rem(e + d, experts), g, t) for d in range(1, experts)]
+    for who in partners:
+        pl.semaphore_signal(barrier, inc=1, device_id=who, device_id_type=MESH)
+    return e, g, t, partners, barrier
+
+
+def one_hot(ei, si, k, capacity, slots):
+    exp = ei[k : k + 1, :]
+    slot = si[k : k + 1, :]
+    target = jnp.where(slot < capacity, exp * capacity + slot, slots)
+    place = lax.broadcasted_iota(jnp.int32, (slots, ei.shape[1]), 0)
+    return place == target
+
+
+def layer_kernel(
+    experts, tok_hbm, grd_hbm, wg_hbm, wu_hbm, wd_hbm, ei, si, prob,
+    out, own, oth, delta, delta_oth,
+    tok, grd, wg, wu, wd, send, got, gate, up, back_grad,
+    part, near, far_out, far, total, back,
+    l_s, w_s, z_s, z_r, x_s, x_r, b_s, b_r, y_s, y_r, o_s, o_r,
+    dy_s, dy_r, n_s, n_r, f_s, f_r, r_s, r_r
+):
+    e, g, t, partners, barrier = greet(experts)
+    sib, opp, other = partners[:3]
+    slots, width = send.shape[2], send.shape[3]
+    half = got.shape[3]
+    share = 2 * width
+    capacity = slots // experts
+    order = (0, 1, 3, 2)
+
+    def window(q):
+        return pl.ds(pl.multiple_of(q * width, width), width)
+
+    def wide(h, q):
+        return pl.ds(pl.multiple_of(h * half + q * width, width), width)
+
+    def rows(s):
+        return pl.ds(pl.multiple_of(s * capacity, 16), capacity)
+
+    loads = []
+    for h in range(2):
+        loads.append(pltpu.make_async_copy(tok_hbm.at[:, wide(h, t)], tok.at[h], l_s.at[0, h]))
+        loads.append(pltpu.make_async_copy(grd_hbm.at[:, wide(h, t)], grd.at[h], l_s.at[1, h]))
+    for copy in loads:
+        copy.start()
+    weights = [
+        pltpu.make_async_copy(wg_hbm.at[0], wg, w_s.at[0]),
+        pltpu.make_async_copy(wu_hbm.at[0], wu, w_s.at[1]),
+        pltpu.make_async_copy(wd_hbm.at[0], wd, w_s.at[2]),
+    ]
+    first = one_hot(ei[...], si[...], 0, capacity, slots)
+    second = one_hot(ei[...], si[...], 1, capacity, slots)
+    both = jnp.where(first | second, 1.0, 0.0).astype(jnp.bfloat16)
+    prob_row = prob[...]
+    slot_prob = jnp.sum(
+        jnp.where(first, prob_row[0:1], 0.0) + jnp.where(second, prob_row[1:2], 0.0),
+        axis=1, keepdims=True,
+    )
+    for copy in loads:
+        copy.wait()
+    for h in range(2):
+        send[0, h] = jnp.dot(both, tok[h], preferred_element_type=jnp.float32).astype(jnp.bfloat16)
+        send[1, h] = (
+            slot_prob * jnp.dot(both, grd[h], preferred_element_type=jnp.float32)
+        ).astype(jnp.bfloat16)
+    pl.semaphore_wait(barrier, len(partners))
+
+    mine, across = window(t), window(opp[2])
+    sends, recvs = [], []
+
+    def remote(src, dst, s_sem, r_sem, who):
+        copy = pltpu.make_async_remote_copy(
+            src_ref=src, dst_ref=dst, send_sem=s_sem, recv_sem=r_sem,
+            device_id=who, device_id_type=MESH,
+        )
+        copy.start()
+        sends.append(copy)
+        return copy
+
+    z, x, b, y = {}, {}, {}, {}
+    for a in range(2):
+        for d in (2, 3, 1):
+            z[d, a] = remote(
+                send.at[a, :, rows(lax.rem(e + d, experts))],
+                got.at[a, :, rows(e), mine],
+                z_s.at[d, a], z_r.at[d, a], partners[2 + d],
+            )
+    for a in range(2):
+        for h in range(2):
+            got[a, h, rows(e), mine] = send[a, h, rows(e)]
+    for copy in weights:
+        copy.start()
+
+    def spread(d, a, i):
+        block = rows(lax.rem(e + experts - d, experts))
+        cols = across if i else mine
+        here = got.at[a, :, block, cols]
+        if i == 0:
+            if d:
+                z[d, a].wait_recv()
+            x[d, a] = remote(here, here, x_s.at[d, a], x_r.at[d, a], opp)
+        else:
+            x[d, a].wait_recv()
+        b[d, a, i] = remote(here, here, b_s.at[d, a, i], b_r.at[d, a, i], sib)
+        y[d, a, i] = remote(
+            got.at[a, 1 - g, block, cols], oth.at[a, block, cols],
+            y_s.at[d, a, i], y_r.at[d, a, i], other,
+        )
+
+    def near_sum(q, start):
+        for ref, w in ((gate, wg), (up, wu)):
+            value = sum(
+                jnp.dot(
+                    got[0, h, :, window(q)], w[wide(h, q), :], preferred_element_type=jnp.float32
+                )
+                for h in range(2)
+            )
+            ref[...] = value if start else ref[...] + value
+
+    def back_sum(q, start):
+        value = sum(
+            lax.dot_general(
+                got[1, h, :, window(q)], wd[:, wide(h, q)], LAST,
+                preferred_element_type=jnp.float32,
+            )
+            for h in range(2)
+        )
+        back_grad[...] = value if start else back_grad[...] + value
+
+    spread(0, 0, 0)
+    spread(0, 1, 0)
+    for d in order[1:]:
+        spread(d, 0, 0)
+    spread(0, 0, 1)
+    for prev, d in zip(order[:3], order[1:]):
+        spread(d, 1, 0)
+        spread(d, 0, 1)
+    weights[0].wait()
+    weights[1].wait()
+    near_sum(t, True)
+    spread(0, 1, 1)
+    for d in order:
+        b[d, 0, 0].wait_recv()
+    near_sum(sib[2], False)
+    spread(1, 1, 1)
+    near_sum(opp[2], False)
+    for d in order:
+        b[d, 0, 1].wait_recv()
+    near_sum(lax.rem(sib[2] + 2, 4), False)
+    spread(3, 1, 1)
+    weights[2].wait()
+    back_sum(t, True)
+    for d in order:
+        b[d, 1, 0].wait_recv()
+    back_sum(sib[2], False)
+    spread(2, 1, 1)
+    back_sum(opp[2], False)
+    for d in order:
+        b[d, 1, 1].wait_recv()
+    back_sum(lax.rem(sib[2] + 2, 4), False)
+
+    keep = pltpu.make_async_copy(got.at[:, g], own, l_s.at[0, 0])
+    keep.start()
+    v, u, k = gate[...], up[...], back_grad[...]
+    sig = jax.nn.sigmoid(v)
+    act = v * sig
+    delta[0] = (k * u * sig * (1.0 + v * (1.0 - sig))).astype(jnp.bfloat16)
+    delta[1] = (k * act).astype(jnp.bfloat16)
+    delta[2] = (act * u).astype(jnp.bfloat16)
+
+    dy = [
+        remote(delta.at[i], delta_oth.at[i], dy_s.at[i], dy_r.at[i], other) for i in range(3)
+    ]
+    tile = width
+    c = lax.rem(t, 2)
+    xi = t // 2
+
+    def product(q):
+        @pl.loop(0, share // tile)
+        def _(i):
+            block = pl.ds(pl.multiple_of(q * share + i * tile, tile), tile)
+            value = lax.dot_general(
+                delta[0], wg[block, :], LAST, preferred_element_type=jnp.float32
+            ) + lax.dot_general(
+                delta[1], wu[block, :], LAST, preferred_element_type=jnp.float32
+            )
+            part[q, :, pl.ds(pl.multiple_of(i * tile, tile), tile)] = value.astype(jnp.bfloat16)
+
+    q_far, q_near = (1 - xi) * 2, xi * 2
+    product(q_far + 1 - c)
+    b_far = remote(part.at[q_far + 1 - c], near.at[0], n_s.at[0], n_r.at[0], sib)
+    product(q_far + c)
+    b_far.wait_recv()
+    back_order = (2, 3, 1, 0)
+    f = {}
+    for d in back_order:
+        block = rows(lax.rem(e + d, experts))
+        far_out[block] = (
+            part[q_far + c, block].astype(jnp.float32) + near[0, block].astype(jnp.float32)
+        ).astype(jnp.bfloat16)
+        f[d] = remote(far_out.at[block], far.at[block], f_s.at[d], f_r.at[d], opp)
+    product(q_near + 1 - c)
+    b_near = remote(part.at[q_near + 1 - c], near.at[1], n_s.at[1], n_r.at[1], sib)
+    product(q_near + c)
+    b_near.wait_recv()
+    r = {}
+    for d in back_order:
+        block = rows(lax.rem(e + d, experts))
+        f[d].wait_recv()
+        value = (
+            part[q_near + c, block].astype(jnp.float32)
+            + near[1, block].astype(jnp.float32)
+            + far[block].astype(jnp.float32)
+        ).astype(jnp.bfloat16)
+        if d:
+            total[block] = value
+            r[d] = remote(total.at[block], back.at[rows(e)], r_s.at[d], r_r.at[d], partners[2 + d])
+        else:
+            back[block] = value
+    for a in range(2):
+        for i in range(2):
+            for d in order:
+                y[d, a, i].wait_recv()
+            here = oth.at[a, :, across if i else mine]
+            recvs.append(remote(here, here, o_s.at[a, i], o_r.at[a, i], sib))
+    keep.wait()
+    for d in (1, 3, 2):
+        r[d].wait_recv()
+    out[...] = lax.dot_general(
+        both, back[...], FIRST, preferred_element_type=jnp.float32
+    ).astype(jnp.bfloat16)
+    for copy in recvs:
+        copy.wait_recv()
+    for copy in dy:
+        copy.wait_recv()
+    for copy in sends:
+        copy.wait_send()
+
+
+VMEM = pl.BlockSpec(memory_space=pltpu.VMEM)
+HBM = pl.BlockSpec(memory_space=pltpu.HBM)
+DMA = pltpu.SemaphoreType.DMA
+
+
+def fast_on_device(
+    tokens, out_grad, expert_index, slot_index, gate_probs, gate_weight, up_weight, down_weight
+):
+    local_rows, model_width = tokens.shape
+    experts = lax.axis_size("expert")
+    slots = 3 * local_rows // 2
+    hidden_part = gate_weight.shape[2]
+    half = model_width // 2
+    width = half // lax.axis_size("tensor")
+    share = model_width // lax.axis_size("tensor")
+    bf = jnp.bfloat16
+    token_grad, got, oth, delta, delta_oth = pl.pallas_call(
+        functools.partial(layer_kernel, experts),
+        out_shape=(
+            jax.ShapeDtypeStruct((local_rows, share), bf),
+            jax.ShapeDtypeStruct((2, slots, half), bf),
+            jax.ShapeDtypeStruct((2, slots, half), bf),
+            jax.ShapeDtypeStruct((3, slots, hidden_part), bf),
+            jax.ShapeDtypeStruct((3, slots, hidden_part), bf),
+        ),
+        in_specs=[HBM] * 5 + [VMEM] * 3,
+        out_specs=(VMEM,) * 5,
+        scratch_shapes=[
+            pltpu.VMEM((2, local_rows, width), bf),
+            pltpu.VMEM((2, local_rows, width), bf),
+            pltpu.VMEM((model_width, hidden_part), bf),
+            pltpu.VMEM((model_width, hidden_part), bf),
+            pltpu.VMEM((hidden_part, model_width), bf),
+            pltpu.VMEM((2, 2, slots, width), bf),
+            pltpu.VMEM((2, 2, slots, half), bf),
+            pltpu.VMEM((slots, hidden_part), jnp.float32),
+            pltpu.VMEM((slots, hidden_part), jnp.float32),
+            pltpu.VMEM((slots, hidden_part), jnp.float32),
+            pltpu.VMEM((4, slots, share), bf),
+            pltpu.VMEM((2, slots, share), bf),
+            pltpu.VMEM((slots, share), bf),
+            pltpu.VMEM((slots, share), bf),
+            pltpu.VMEM((slots, share), bf),
+            pltpu.VMEM((slots, share), bf),
+            DMA((2, 2)), DMA((3,)),
+            DMA((experts, 2)), DMA((experts, 2)),
+            DMA((experts, 2)), DMA((experts, 2)),
+            DMA((experts, 2, 2)), DMA((experts, 2, 2)),
+            DMA((experts, 2, 2)), DMA((experts, 2, 2)),
+            DMA((2, 2)), DMA((2, 2)),
+            DMA((3,)), DMA((3,)),
+            DMA((2,)), DMA((2,)),
+            DMA((experts,)), DMA((experts,)),
+            DMA((experts,)), DMA((experts,)),
+        ],
+        compiler_params=pltpu.CompilerParams(
+            collective_id=0, has_side_effects=True, vmem_limit_bytes=54 * 1024 * 1024
+        ),
+        name="layer",
+    )(
+        tokens, out_grad, gate_weight, up_weight, down_weight,
+        expert_index.T, slot_index.T, gate_probs.T,
+    )
+
+    def grads_kernel(got_ref, oth_ref, delta_ref, delta_oth_ref, gg, ug, dg):
+        i = pl.program_id(0)
+        n = gg.shape[0]
+        cols = pl.ds(pl.multiple_of(i * n, n), n)
+
+        def both(a_own, a_oth, b_own, b_oth):
+            return (
+                lax.dot_general(a_own, b_own, FIRST, preferred_element_type=jnp.float32)
+                + lax.dot_general(a_oth, b_oth, FIRST, preferred_element_type=jnp.float32)
+            ).astype(bf)
+
+        tok_own, tok_oth = got_ref[0, :, cols], oth_ref[0, :, cols]
+        gg[...] = both(tok_own, tok_oth, delta_ref[0], delta_oth_ref[0])
+        ug[...] = both(tok_own, tok_oth, delta_ref[1], delta_oth_ref[1])
+        dg[...] = both(delta_ref[2], delta_oth_ref[2], got_ref[1, :, cols], oth_ref[1, :, cols])
+
+    tile = 512
+    gate_grad, up_grad, down_grad = pl.pallas_call(
+        grads_kernel,
+        grid=(half // tile,),
+        out_shape=(
+            jax.ShapeDtypeStruct((half, hidden_part), bf),
+            jax.ShapeDtypeStruct((half, hidden_part), bf),
+            jax.ShapeDtypeStruct((hidden_part, half), bf),
+        ),
+        in_specs=[VMEM] * 4,
+        out_specs=(
+            pl.BlockSpec((tile, hidden_part), lambda i: (i, 0)),
+            pl.BlockSpec((tile, hidden_part), lambda i: (i, 0)),
+            pl.BlockSpec((hidden_part, tile), lambda i: (0, i)),
+        ),
+        compiler_params=pltpu.CompilerParams(vmem_limit_bytes=48 * 1024 * 1024),
+        name="weight_grads",
+    )(got, oth, delta, delta_oth)
+    return (token_grad, gate_grad[None], up_grad[None], down_grad[None])
 
 
 def on_device(
@@ -116,8 +473,23 @@
 
 
 def solution(mesh):
+    sizes = dict(mesh.shape)
+
+    def body(*args):
+        local_rows, model_width = args[0].shape
+        capacity = 3 * local_rows // (2 * sizes["expert"])
+        fits = (
+            sizes["expert"] == 4
+            and sizes["dp"] == 2
+            and sizes["tensor"] == 4
+            and capacity % 16 == 0
+            and model_width % 4096 == 0
+            and args[5].shape[2] % 256 == 0
+        )
+        return fast_on_device(*args) if fits else on_device(*args)
+
     return jax.shard_map(
-        on_device,
+        body,
         mesh=mesh,
         in_specs=(
             P(("expert", "dp"), None),

time: 196 us -> 62.3 us (0.32)
  blocking collectives: 67.7 us -> 0 us
  Pallas kernels: 0 us -> 55.5 us
  waiting for transfers between devices: 35.6 us -> 0 us
  matrix products: 26.8 us -> 0 us
  other arithmetic: 21.6 us -> 0 us
  between operations: 14 us -> 0.65 us
  starting transfers between devices: 13.2 us -> 0 us
  local copies, waits for them, and re-layouts: 16.4 us -> 5.64 us
    pallas_call x0 -> x2, Pallas kernels: none -> 55.5 us  [the longest x1 50.5 us: fast_on_device(): pl.pallas_call(functools.partial(layer_kernel, experts), out_shape=(jax.S...]
    all_gather x3 -> x0, blocking collectives: 35.9 us -> none  [the longest x1 22.7 us: on_device(): piece_gate = lax.all_gather(gate_delta, 'dp', axis=0, tiled=True)]
    all_to_all x2 -> x0, blocking collectives: 31.8 us -> none  [the longest x1 17.9 us: on_device(): lax.all_to_all(token_share, 'expert', split_axis=0, concat_axis=0, tiled=...]
    dot_general x8 -> x0, matrix products: 26.8 us -> none  [the longest x3 12.4 us: rounded_sum(): product = jnp.einsum(form, left, right, preferred_element_type=jnp.float32)]
    all_to_all x3 -> x0, waiting for transfers between devices: 18.7 us -> none  [the longest x1 18.7 us: on_device(): lax.all_to_all(scaled, 'dp', split_axis=1, concat_axis=0, tiled=True)]
    reduce_sum x4 -> x0, other arithmetic: 18.3 us -> none  [the longest x3 14.9 us: rounded_sum(): jnp.sum(lax.optimization_barrier(product.astype(jnp.bfloat16)).astype(jnp...]
    all_gather x2 -> x0, waiting for transfers between devices: 16.9 us -> none  [the longest x1 16.9 us: on_device(): lax.all_gather(grad_share, 'tensor', axis=1, tiled=True)]
    all_to_all x3 -> x0, starting transfers between devices: 13.1 us -> none  [the longest x1 4.83 us: on_device(): lax.all_to_all(scaled, 'dp', split_axis=1, concat_axis=0, tiled=True)]
  transfers between devices with their start and end apart: 6 -> 0, of which waited for: 2 -> 0; matrix products, arithmetic and copies ran while one was open for 21% -> 0% of each run, Pallas kernels for 0% -> 0%
where the time goes in v2:
time: 62.3 us; the launch traced here: 61.8 us
  Pallas kernels  55.5 us (89%)
  local copies, waits for them, and re-layouts  5.64 us (9%)
  between operations  0.65 us (1%)
    pallas_call x1, Pallas kernels, fast_on_device(): pl.pallas_call(functools.partial(layer_kernel, experts), out_shape=(jax.S...  50.5 us
    unnamed x11, local copies, waits for them, and re-layouts  5.64 us
    pallas_call x1, Pallas kernels, fast_on_device(): pl.pallas_call(grads_kernel, grid=(half // tile,), out_shape=(jax.ShapeDt...  5 us

profile of v2, /device:TPU:0, one launch (start us, length us, event | category | flops | bytes accessed | tf_op | source)
XLA Modules:
  0.0 61.8 jit_solution(16002780124079753080)
XLA Ops:
  0.6 50.5 %layer.1 = (bf16[128,1024]{1,0:T(8,128)(2,1)}, bf16[2,192,2048]{2,1,0:T(8,128)(2,1)}, bf16[2,192,2048]{2,1,0:T(8,128)(2,1)}, bf16[3,192,512]{2,1,0:T(8,128)(2,1)}, bf16[3,192,512]{2,1,0:T(8,128)(2,1)}) custom-call(bf16[128,4096]{1,0:T(8,128)(2,1)} %tok_hbm.1, bf16[128,4096]{1,0:T(8,128)(2,1)} %grd_hbm.1, bf16[1,4096,512]{2,1,0:T(8,128)(2,1)} %wg_hbm.1, ...), custom_call_target="tpu_custom_call" | custom-call | tf_op jit(solution)/shard_map/layer/pallas_call | solution.py:279
  51.1 0.0 copy-start
  51.1 1.4 %copy-done = bf16[2,192,2048]{2,1,0:T(8,128)(2,1)S(1)} copy-done((bf16[2,192,2048]{2,1,0:T(8,128)(2,1)S(1)}, bf16[2,192,2048]{2,1,0:T(8,128)(2,1)}, u32[]{:S(2)}) %copy-start) | copy-done | bytes 1572888
  52.5 0.0 copy-start.1
  52.5 1.4 %copy-done.1 = bf16[2,192,2048]{2,1,0:T(8,128)(2,1)S(1)} copy-done((bf16[2,192,2048]{2,1,0:T(8,128)(2,1)S(1)}, bf16[2,192,2048]{2,1,0:T(8,128)(2,1)}, u32[]{:S(2)}) %copy-start.1) | copy-done | bytes 1572888
  53.9 0.0 copy-start.2
  53.9 1.1 %copy-done.2 = bf16[3,192,512]{2,1,0:T(8,128)(2,1)S(1)} copy-done((bf16[3,192,512]{2,1,0:T(8,128)(2,1)S(1)}, bf16[3,192,512]{2,1,0:T(8,128)(2,1)}, u32[]{:S(2)}) %copy-start.2) | copy-done | bytes 589848
  55.0 0.0 copy-start.3
  55.0 1.1 %copy-done.3 = bf16[3,192,512]{2,1,0:T(8,128)(2,1)S(1)} copy-done((bf16[3,192,512]{2,1,0:T(8,128)(2,1)S(1)}, bf16[3,192,512]{2,1,0:T(8,128)(2,1)}, u32[]{:S(2)}) %copy-start.3) | copy-done | bytes 589848
  56.1 0.0 copy-start.4
  56.1 5.0 %weight_grads.1 = (bf16[2048,512]{1,0:T(8,128)(2,1)}, bf16[2048,512]{1,0:T(8,128)(2,1)}, bf16[512,2048]{1,0:T(8,128)(2,1)}) custom-call(bf16[2,192,2048]{2,1,0:T(8,128)(2,1)S(1)} %copy-done, bf16[2,192,2048]{2,1,0:T(8,128)(2,1)S(1)} %copy-done.1, bf16[3,192,512]{2,1,0:T(8,128)(2,1)S(1)} %copy-done.2, bf16[3,192,512]{2,1,0:T(8,128)(2,1)S(1)} %copy-done.3), custom_call_target="tpu_custom_call" | custom-call | tf_op jit(solution)/shard_map/weight_grads/pallas_call | solution.py:344
  61.0 0.0 copy-done.4
  61.1 0.7 %copy.13 = bf16[128,1024]{1,0:T(8,128)(2,1)} copy(bf16[128,1024]{1,0:T(8,128)(2,1)S(1)} %copy-done.4) | data formatting | bytes 524288
Async XLA Ops:
  51.1 1.4 %copy-start = (bf16[2,192,2048]{2,1,0:T(8,128)(2,1)S(1)}, bf16[2,192,2048]{2,1,0:T(8,128)(2,1)}, u32[]{:S(2)}) copy-start(bf16[2,192,2048]{2,1,0:T(8,128)(2,1)} %get-tuple-element.13.got_ref) | copy-start | bytes 4718596
  52.5 1.4 %copy-start.1 = (bf16[2,192,2048]{2,1,0:T(8,128)(2,1)S(1)}, bf16[2,192,2048]{2,1,0:T(8,128)(2,1)}, u32[]{:S(2)}) copy-start(bf16[2,192,2048]{2,1,0:T(8,128)(2,1)} %get-tuple-element.14.oth_ref) | copy-start | bytes 4718596
  53.9 1.1 %copy-start.2 = (bf16[3,192,512]{2,1,0:T(8,128)(2,1)S(1)}, bf16[3,192,512]{2,1,0:T(8,128)(2,1)}, u32[]{:S(2)}) copy-start(bf16[3,192,512]{2,1,0:T(8,128)(2,1)} %get-tuple-element.15.delta_ref) | copy-start | bytes 1769476
  55.0 1.1 %copy-start.3 = (bf16[3,192,512]{2,1,0:T(8,128)(2,1)S(1)}, bf16[3,192,512]{2,1,0:T(8,128)(2,1)}, u32[]{:S(2)}) copy-start(bf16[3,192,512]{2,1,0:T(8,128)(2,1)} %get-tuple-element.16.delta_oth_ref) | copy-start | bytes 1769476
  56.1 5.0 %copy-start.4 = (bf16[128,1024]{1,0:T(8,128)(2,1)S(1)}, bf16[128,1024]{1,0:T(8,128)(2,1)}, u32[]{:S(2)}) copy-start(bf16[128,1024]{1,0:T(8,128)(2,1)} %get-tuple-element.24) | copy-start | bytes 786436
